TPU v7x, 32 devices: a whole 2x2x4 slice. The times are simulated.
32 devices in a mesh: rows: 16 (over z, y, x), blk: 2 (over core).
Axes of the slice: x: 2, y: 2, z: 4, core: 2. Of those that a mesh axis runs over, the one named last changes fastest.
Arguments:
- inputs: bfloat16 [16384, 440], P('rows'), may hold values from -6 to 6
- proj: bfloat16 [4, 440, 512], P('blk'), may hold values from -0.25 to 0.25
- phase: bfloat16 [4, 512], P('blk'), may hold values from -3.140625 to 3.140625
- targets: bfloat16 [16384, 1024], P('rows', 'blk'), may hold values from -6 to 6
Outputs:
- coefs: float32 [4, 512, 1024], P(None, None, 'blk')
- residual: float32 [16384, 1024], P('rows', 'blk')
All inputs are finite; a program needn't handle non-finite values.
Results may differ from a plain program's by a relative error of at most 0.0035.
The roundings to bfloat16 on the way count: a program that leaves them out, or rounds other values in their place, can miss the bound.
Values may be sent and summed in bfloat16 or wider, within the bound.
No kernel may reach another device: no remote copies, remote signals or barrier semaphores. Data moves between devices by JAX's collectives and lax.ppermute only.
A program may use at most 128 MiB of HBM per device.

v0:
```python
import math

import jax
import jax.numpy as jnp
from jax import lax
from jax.sharding import PartitionSpec as P

ridge = 0.05


def broadcast(value, axis, root):
    mine = lax.axis_index(axis) == root
    return lax.psum(jnp.where(mine, value, jnp.zeros_like(value)), axis)


def build(inputs, weights, shift, factor_scale):
    pre = jnp.dot(inputs, weights, preferred_element_type=jnp.float32) + shift.astype(jnp.float32)
    return (jnp.cos(pre) * factor_scale).astype(jnp.bfloat16)


def body(inputs, proj, phase, targets):
    local_rows = inputs.shape[0]
    factor_scale = 1.0 / math.sqrt(local_rows * lax.axis_size("rows"))
    owned = proj.shape[0]
    width = proj.shape[2]
    feat_list = [build(inputs, proj[index], phase[index], factor_scale) for index in range(owned)]
    gram_list = [
        lax.dot_general(feats, feats, (((0,), (0,)), ((), ())), preferred_element_type=jnp.float32)
        for feats in feat_list
    ]
    summed = lax.psum(tuple(gram_list), "rows")
    identity_mat = jnp.eye(width, dtype=jnp.float32)
    own_factors = jnp.stack([jnp.linalg.cholesky(gram + ridge * identity_mat) for gram in summed])
    factors = lax.all_gather(own_factors, "blk", axis=0, tiled=True)
    total_blocks = owned * lax.axis_size("blk")
    residual = targets.astype(jnp.float32)
    coef_list = []
    for block in range(total_blocks):
        owner = block // owned
        local = block % owned
        feats = broadcast(feat_list[local], "blk", owner)
        partial_corr = lax.dot_general(
            feats,
            residual.astype(jnp.bfloat16),
            (((0,), (0,)), ((), ())),
            preferred_element_type=jnp.float32,
        )
        factor = factors[block]
        corr = lax.psum(partial_corr, "rows")
        delta = jax.scipy.linalg.cho_solve((factor, True), corr)
        coef_list.append(delta)
        residual = residual - jnp.dot(
            feats, delta.astype(jnp.bfloat16), preferred_element_type=jnp.float32
        )
    return (jnp.stack(coef_list), residual)


def solution(mesh):
    return jax.shard_map(
        body,
        mesh=mesh,
        in_specs=(P("rows", None), P("blk", None, None), P("blk", None), P("rows", "blk")),
        out_specs=(P(None, None, "blk"), P("rows", "blk")),
        check_vma=False,
    )
```

profile of v0, /device:TPU:0, one launch (start us, length us, event | category | flops | bytes accessed | tf_op | source)
XLA Modules:
  0.0 863.6 jit_solution(6765162097738033540)
XLA Ops:
  8.4 9.9 %broadcast_select_fusion.1 = (bf16[1024,512]{1,0:T(8,128)(2,1)}, bf16[1024,512]{1,0:T(8,128)(2,1)}, bf16[1024,512]{1,0:T(8,128)(2,1)S(1)}) fusion(pred[]{:T(512)S(6)} %eq.15, pred[]{:T(512)S(6)} %eq.14, f32[512]{0:T(512)S(1)} %bitcast.240, bf16[1024,440]{0,1:T(8,128)(2,1)S(1)} %copy-done, bf16[2,440,512]{2,1,0:T(8,128)(2,1)} %param.8), kind=kOutput, calls=%fused_computation.81 | convolution fusion | flops 463994880 | bytes 4499458 | tf_op jit(solution)/shard_map/dot_general | solution.py:17
  31.4 28.1 %all-reduce.17.cloned.1.call-done = (bf16[1024,512]{1,0:T(8,128)(2,1)}, bf16[1024,512]{1,0:T(8,128)(2,1)}, bf16[1024,512]{1,0:T(8,128)(2,1)}, bf16[1024,512]{1,0:T(8,128)(2,1)}) async-done(((bf16[1024,512]{1,0:T(8,128)(2,1)}, bf16[1024,512]{1,0:T(8,128)(2,1)}, bf16[1024,512]{1,0:T(8,128)(2,1)}, bf16[1024,512]{1,0:T(8,128)(2,1)}), (bf16[1024,512]{1,0:T(8,128)(2,1)}, bf16[1024,512]{1,0:T(8,128)(2,1)}, ...) | async-done | bytes 4194320 | tf_op jit(solution)/shard_map/psum | solution.py:13
  63.0 153.0 %all-reduce.15.cloned.1.call-done = (f32[512,512]{1,0:T(8,128)}, f32[512,512]{0,1:T(8,128)}, f32[512,512]{0,1:T(8,128)}) async-done(((f32[512,512]{1,0:T(8,128)}, f32[512,512]{0,1:T(8,128)}, f32[512,512]{0,1:T(8,128)}), (f32[512,512]{1,0:T(8,128)}, f32[512,512]{0,1:T(8,128)}, f32[512,512]{0,1:T(8,128)})) %all-reduce.15.cloned.1.call-update) | async-done | bytes 3145744 | tf_op jit(solution)/shard_map/psum | solution.py:49
  222.0 11.7 %cholesky.286 = f32[128,128]{1,0:T(8,128)S(1)} custom-call(f32[128,128]{1,0:T(8,128)S(1)} %cholesky.426), custom_call_target="Cholesky" | custom-call | tf_op jit(solution)/shard_map/jit(cholesky)/cholesky | solution.py:33
  233.8 9.8 %custom-call.31 = f32[1,128,128]{1,2,0:T(8,128)S(1)} custom-call(f32[1,128,128]{2,1,0:T(8,128)S(1)} %get-tuple-element.98), custom_call_target="InvertDiagBlocksLowerTriangular" | custom-call | tf_op jit(solution)/shard_map/jit(cholesky)/cholesky | solution.py:33
  246.2 11.7 %cholesky.305 = f32[128,128]{1,0:T(8,128)S(1)} custom-call(f32[128,128]{1,0:T(8,128)S(1)} %cholesky.430), custom_call_target="Cholesky" | custom-call | tf_op jit(solution)/shard_map/jit(cholesky)/cholesky | solution.py:33
  259.3 9.9 %custom-call.32 = f32[1,128,128]{1,2,0:T(8,128)S(1)} custom-call(f32[1,128,128]{2,1,0:T(8,128)S(1)} %get-tuple-element.95), custom_call_target="InvertDiagBlocksLowerTriangular" | custom-call | tf_op jit(solution)/shard_map/jit(cholesky)/cholesky | solution.py:33
  270.8 11.7 %cholesky.326 = f32[128,128]{1,0:T(8,128)S(1)} custom-call(f32[128,128]{1,0:T(8,128)S(1)} %cholesky.435), custom_call_target="Cholesky" | custom-call | tf_op jit(solution)/shard_map/jit(cholesky)/cholesky | solution.py:33
  294.5 11.9 %cholesky.343 = f32[128,128]{1,0:T(8,128)S(1)} custom-call(f32[128,128]{1,0:T(8,128)S(1)} %convolution_subtract_fusion.32), custom_call_target="Cholesky" | custom-call | tf_op jit(solution)/shard_map/jit(cholesky)/cholesky | solution.py:33
  311.1 11.7 %cholesky.358 = f32[128,128]{1,0:T(8,128)S(1)} custom-call(f32[128,128]{1,0:T(8,128)S(1)} %cholesky.439), custom_call_target="Cholesky" | custom-call | tf_op jit(solution)/shard_map/jit(cholesky)/cholesky | solution.py:33
  335.4 11.7 %cholesky.377 = f32[128,128]{1,0:T(8,128)S(1)} custom-call(f32[128,128]{1,0:T(8,128)S(1)} %cholesky.443), custom_call_target="Cholesky" | custom-call | tf_op jit(solution)/shard_map/jit(cholesky)/cholesky | solution.py:33
  348.4 10.2 %custom-call.35 = f32[1,128,128]{1,2,0:T(8,128)S(1)} custom-call(f32[1,128,128]{2,1,0:T(8,128)S(1)} %get-tuple-element.105), custom_call_target="InvertDiagBlocksLowerTriangular" | custom-call | tf_op jit(solution)/shard_map/jit(cholesky)/cholesky | solution.py:33
  360.1 11.7 %cholesky.398 = f32[128,128]{1,0:T(8,128)S(1)} custom-call(f32[128,128]{1,0:T(8,128)S(1)} %cholesky.448), custom_call_target="Cholesky" | custom-call | tf_op jit(solution)/shard_map/jit(cholesky)/cholesky | solution.py:33
  383.8 11.7 %cholesky.415 = f32[128,128]{1,0:T(8,128)S(1)} custom-call(f32[128,128]{1,0:T(8,128)S(1)} %convolution_subtract_fusion.31), custom_call_target="Cholesky" | custom-call | tf_op jit(solution)/shard_map/jit(cholesky)/cholesky | solution.py:33
  404.1 12.7 %all-gather.2.cloned.1.call-done = f32[4,512,512]{2,1,0:T(8,128)} async-done(((f32[2,512,512]{2,1,0:T(8,128)}), f32[4,512,512]{2,1,0:T(8,128)}) %all-gather.2.cloned.1.call-update) | async-done | bytes 4194320 | tf_op jit(solution)/shard_map/all_gather | solution.py:34
  429.1 39.3 %custom-call.37 = f32[4,128,128]{1,2,0:T(8,128)S(1)} custom-call(f32[4,128,128]{2,1,0:T(8,128)S(1)} %get-tuple-element.30), custom_call_target="InvertDiagBlocksLowerTriangular" | custom-call | tf_op jit(solution)/shard_map/jit(_cho_solve)/triangular_solve | solution.py:50
  478.1 11.9 %while.9 = (s32[]{:T(128)}, f32[512,512]{1,0:T(8,128)}, s32[4,2]{0,1:T(2,128)S(1)}, f32[4,128,128]{2,1,0:T(8,128)S(1)}, s32[]{:T(128)}) while((s32[]{:T(128)}, f32[512,512]{1,0:T(8,128)}, s32[4,2]{0,1:T(2,128)S(1)}, f32[4,128,128]{2,1,0:T(8,128)S(1)}, s32[]{:T(128)}) %tuple.118), condition=%wide.while_cond.clone, body=%wide.while_body.clone.sunk | while | flops 2 | bytes 131181 | solution.py:50
  490.0 39.3 %custom-call.38 = f32[4,128,128]{1,2,0:T(8,128)S(1)} custom-call(f32[4,128,128]{2,1,0:T(8,128)S(1)} %get-tuple-element.31), custom_call_target="InvertDiagBlocksLowerTriangular" | custom-call | tf_op jit(solution)/shard_map/jit(_cho_solve)/triangular_solve | solution.py:50
  529.3 62.0 %all-reduce.9.cloned.1.call-done = f32[512,512]{1,0:T(8,128)} async-done(((f32[512,512]{1,0:T(8,128)}), f32[512,512]{1,0:T(8,128)}) %all-reduce.9.cloned.1.call-update) | async-done | bytes 1048592 | tf_op jit(solution)/shard_map/psum | solution.py:49
  613.4 39.3 %custom-call.39 = f32[4,128,128]{1,2,0:T(8,128)S(1)} custom-call(f32[4,128,128]{2,1,0:T(8,128)S(1)} %get-tuple-element.32), custom_call_target="InvertDiagBlocksLowerTriangular" | custom-call | tf_op jit(solution)/shard_map/jit(_cho_solve)/triangular_solve | solution.py:50
  652.7 64.1 %all-reduce.11.cloned.1.call-done = f32[512,512]{1,0:T(8,128)} async-done(((f32[512,512]{1,0:T(8,128)}), f32[512,512]{1,0:T(8,128)}) %all-reduce.11.cloned.1.call-update) | async-done | bytes 1048592 | tf_op jit(solution)/shard_map/psum | solution.py:49
  729.0 14.3 %while.11 = (s32[]{:T(128)}, f32[512,512]{1,0:T(8,128)}, s32[4,2]{0,1:T(2,128)S(1)}, f32[4,128,128]{2,1,0:T(8,128)}, s32[]{:T(128)}) while((s32[]{:T(128)}, f32[512,512]{1,0:T(8,128)}, s32[4,2]{0,1:T(2,128)S(1)}, f32[4,128,128]{2,1,0:T(8,128)}, s32[]{:T(128)}) %tuple.120), condition=%wide.while_cond.clone.2, body=%wide.while_body.clone.2.sunk | while | flops 2 | bytes 132705 | solution.py:50
  743.3 41.0 %custom-call.40 = f32[4,128,128]{1,2,0:T(8,128)} custom-call(f32[4,128,128]{2,1,0:T(8,128)} %get-tuple-element.33), custom_call_target="InvertDiagBlocksLowerTriangular" | custom-call | tf_op jit(solution)/shard_map/jit(_cho_solve)/triangular_solve | solution.py:50
  788.6 51.3 %all-reduce.13.cloned.1.call-done = f32[512,512]{1,0:T(8,128)} async-done(((f32[512,512]{1,0:T(8,128)}), f32[512,512]{1,0:T(8,128)}) %all-reduce.13.cloned.1.call-update) | async-done | bytes 1048592 | tf_op jit(solution)/shard_map/psum | solution.py:49
  (269 shorter events, 194.5 us)
Async XLA Ops:
  7.2 52.3 %all-reduce.17.cloned.1.call-start = ((), (), s32[]{:S(2)}) async-start(), calls=%async_computation.5 | async-start | bytes 8388608 | tf_op jit(solution)/shard_map/psum | solution.py:13
  8.4 9.9 %copy-start.39 = (bf16[2,440,512]{2,1,0:T(8,128)(2,1)S(1)}, bf16[2,440,512]{2,1,0:T(8,128)(2,1)}, u32[]{:S(2)}) copy-start(bf16[2,440,512]{2,1,0:T(8,128)(2,1)} %param.8) | copy-start | bytes 2703364
  27.9 188.2 %all-reduce.15.cloned.1.call-start = ((), (), s32[]{:S(2)}) async-start(), calls=%async_computation.4 | async-start | bytes 6291456 | tf_op jit(solution)/shard_map/psum | solution.py:49
  29.7 29.8 %copy-start.32 = (bf16[1024,512]{1,0:T(8,128)(2,1)S(1)}, bf16[1024,512]{1,0:T(8,128)(2,1)}, u32[]{:S(2)}) copy-start(bf16[1024,512]{1,0:T(8,128)(2,1)} %param.10) | copy-start | bytes 3145732
  62.4 354.4 %all-gather.2.cloned.1.call-start = ((), (), s32[]{:S(2)}) async-start(), calls=%async_computation | async-start | bytes 6291456 | tf_op jit(solution)/shard_map/all_gather | solution.py:34
  399.9 2.6 copy-start.10
  404.1 187.2 %all-reduce.9.cloned.1.call-start = ((), (), s32[]{:S(2)}) async-start(), calls=%async_computation.1 | async-start | bytes 2097152 | tf_op jit(solution)/shard_map/psum | solution.py:49
  404.1 64.3 %copy-start.37 = (f32[512,512]{1,0:T(8,128)S(1)}, f32[512,512]{1,0:T(8,128)}, u32[]{:S(2)}) copy-start(f32[512,512]{1,0:T(8,128)} %get-tuple-element.66) | copy-start | bytes 3145732
  472.4 2.3 copy-start.33
  472.4 2.3 copy-start.34
  477.8 239.0 %all-reduce.11.cloned.1.call-start = ((), (), s32[]{:S(2)}) async-start(), calls=%async_computation.2 | async-start | bytes 2097152 | tf_op jit(solution)/shard_map/psum | solution.py:49
  591.3 3.3 copy-start.8
  605.4 234.5 %all-reduce.13.cloned.1.call-start = ((), (), s32[]{:S(2)}) async-start(), calls=%async_computation.3 | async-start | bytes 2097152 | tf_op jit(solution)/shard_map/psum | solution.py:49
  716.8 3.2 copy-start.38
  722.8 2.3 copy-start.3
  722.8 2.3 copy-start.19
  723.2 2.7 copy-start.4
  784.3 3.3 copy-start.5
  784.3 3.3 copy-start.15
  784.3 3.2 copy-start.31
  786.5 53.4 %copy-start.35 = (f32[4,128,128]{1,2,0:T(8,128)S(1)}, f32[4,128,128]{1,2,0:T(8,128)}, u32[]{:S(2)}) copy-start(f32[4,128,128]{1,2,0:T(8,128)} %custom-call.40) | copy-start | bytes 786436
  839.9 5.2 copy-start.6
  842.7 4.4 copy-start.36
  853.8 2.5 copy-start.1
  (22 other events, 34.8 us)
Sparse Core Ops, SparseCore 0:
  28.0 31.4 all-reduce.16
  67.1 148.9 all-reduce.14
  404.2 12.6 all-gather.1
  478.0 113.2 all-reduce.8
  605.5 111.2 all-reduce.10
  728.3 111.4 all-reduce.12
where the time goes:
time: 870 us; the launch traced here: 864 us
  waiting for transfers between devices  371 us (43%)
  other arithmetic  337 us (39%)
  matrix products  80.8 us (9%)
  local copies, waits for them, and re-layouts  52.2 us (6%)
  between operations  20.7 us (2%)
    psum x4, waiting for transfers between devices, body(): corr = lax.psum(partial_corr, 'rows')  330 us
    another operation x6, other arithmetic, body(): delta = jax.scipy.linalg.cho_solve((factor, True), corr)  163 us
    another operation x30, other arithmetic, body(): jnp.linalg.cholesky(gram + ridge * identity_mat)  159 us
    another operation x53, local copies, waits for them, and re-layouts, body(): delta = jax.scipy.linalg.cho_solve((factor, True), corr)  42.4 us
    another operation x56, matrix products, body(): delta = jax.scipy.linalg.cho_solve((factor, True), corr)  34.4 us
    psum x1, waiting for transfers between devices, broadcast(): return lax.psum(jnp.where(mine, value, jnp.zeros_like(value)), axis)  28.1 us
    dot_general x2, matrix products, build(): jnp.dot(inputs, weights, preferred_element_type=jnp.float32)  19.5 us
  transfers between devices with their start and end apart: 6, of which 6 were waited for; matrix products, arithmetic and copies ran while one was open for 19% of the time, Pallas kernels for 0%

commit v1 on v0

v1 whole, which is shorter than its diff:
```python
import functools
import math

import jax
import jax.numpy as jnp
from jax import lax
from jax.experimental import pallas as pl
from jax.experimental.pallas import tpu as pltpu
from jax.sharding import PartitionSpec as P

ridge = 0.05
wire = jnp.float16
HI = lax.Precision.HIGHEST
f32, bf16 = jnp.float32, jnp.bfloat16

PI_A, PI_B, PI_C = 3.140625, 9.67502593994140625e-4, 1.509957990978376432e-7
SIN = (0.9999999956905781, -0.16666657923140904, 0.008333049389622973, -0.000198089486478871, 2.604931690728071e-06)
VMEM = 50 * 1024 * 1024


def cosine(x):
    whole = jnp.floor(x * (1.0 / math.pi))
    shift = whole + 0.5
    r = ((x - shift * PI_A) - shift * PI_B) - shift * PI_C
    u = r * r
    p = SIN[4]
    for c in SIN[3::-1]:
        p = p * u + c
    s = r * p
    odd = (whole.astype(jnp.int32) & 1) == 1
    return jnp.where(odd, s, -s)


def features_kernel(scale, x_ref, w_ref, p_ref, o_ref):
    pre = jnp.dot(x_ref[...], w_ref[0], preferred_element_type=f32) + p_ref[0].astype(f32)
    o_ref[0] = (cosine(pre) * scale).astype(bf16)


def features(x, w, p, scale):
    rows, depth = x.shape
    blocks, _, width = w.shape
    tile = min(rows, 256)
    return pl.pallas_call(
        functools.partial(features_kernel, scale),
        grid=(blocks, rows // tile),
        in_specs=[
            pl.BlockSpec((tile, depth), lambda b, i: (i, 0)),
            pl.BlockSpec((1, depth, width), lambda b, i: (b, 0, 0)),
            pl.BlockSpec((1, 1, width), lambda b, i: (b, 0, 0)),
        ],
        out_specs=pl.BlockSpec((1, tile, width), lambda b, i: (b, i, 0)),
        out_shape=jax.ShapeDtypeStruct((blocks, rows, width), bf16),
        compiler_params=pltpu.CompilerParams(vmem_limit_bytes=VMEM),
        name="features",
    )(x, w, p.reshape(blocks, 1, width))


def split(a):
    hi = a.astype(bf16)
    return hi, (a - hi.astype(f32)).astype(bf16)


def dot1(a, b):
    return jnp.dot(a, b, preferred_element_type=f32)


def dot3(a, b):
    ah, al = split(a)
    bh, bl = split(b)
    return dot1(ah, bh) + (dot1(ah, bl) + dot1(al, bh))


def dot6(a, b):
    return jnp.dot(a, b, precision=HI, preferred_element_type=f32)


def tdot6(a, b):
    return lax.dot_general(a, b, (((0,), (0,)), ((), ())), precision=HI, preferred_element_type=f32)


def eye(n):
    return (lax.broadcasted_iota(jnp.int32, (n, n), 0) == lax.broadcasted_iota(jnp.int32, (n, n), 1)).astype(f32)


def invert(a_refs, x_refs):
    n = a_refs[0].shape[-1]
    top = jnp.float32(0.0)
    for a in a_refs:
        top = jnp.maximum(top, jnp.max(jnp.sum(jnp.abs(a[...]), axis=1)))
    top = top * 1.0001
    ident = eye(n)
    for x in x_refs:
        x[...] = ident * (1.0 / top)

    def step(low):
        scale = 2.0 / (1.0 + low)
        for a, x in zip(a_refs, x_refs):
            xv = x[...] * scale
            y = dot3(a[...], xv)
            x[...] = 2.0 * xv - dot3(xv, y)
        return jnp.minimum(4.0 * low / ((1.0 + low) * (1.0 + low)) * 0.999, 1.0)

    lax.while_loop(lambda low: low < 0.98, step, 0.9 * ridge / top)
    for a, x in zip(a_refs, x_refs):
        xv = x[...]
        x[...] = 2.0 * xv - dot6(xv, dot6(a[...], xv))


def factor_kernel(inv_n, g_ref, s_ref, o_ref, a_ref, t_ref, v_ref, x_ref, y_ref):
    blocks, width, _ = g_ref.shape
    h = width // 2
    every = range(blocks)
    for b in every:
        s = s_ref[b]
        full = g_ref[b] + tdot6(s, s) * inv_n + ridge * eye(width)
        a_ref[b] = full[:h, :h]
        t_ref[b] = full[h:, :h]
        v_ref[b] = full[h:, h:]
    invert([a_ref.at[b] for b in every], [x_ref.at[b] for b in every])
    for b in every:
        t = t_ref[b]
        v = dot6(t, x_ref[b])
        t_ref[b] = v
        a_ref[b] = v_ref[b] - lax.dot_general(v, t, (((1,), (1,)), ((), ())), precision=HI, preferred_element_type=f32)
    invert([a_ref.at[b] for b in every], [y_ref.at[b] for b in every])
    for b in every:
        v, y = t_ref[b], y_ref[b]
        low = dot6(y, v)
        o_ref[b, h:, h:] = y
        o_ref[b, h:, :h] = -low
        o_ref[b, :h, h:] = -low.T
        o_ref[b, :h, :h] = x_ref[b] + tdot6(v, low)


def factor(g, s, n):
    blocks, width, _ = g.shape
    h = width // 2
    half = pltpu.VMEM((blocks, h, h), f32)
    return pl.pallas_call(
        functools.partial(factor_kernel, 1.0 / n),
        out_shape=jax.ShapeDtypeStruct(g.shape, f32),
        scratch_shapes=[half] * 5,
        compiler_params=pltpu.CompilerParams(vmem_limit_bytes=VMEM),
        name="factor",
    )(g, s)


def solve_kernel(inv_n, pairs, w_ref, x_ref, s_ref, t_ref, c_ref, o_ref, d_ref):
    blocks = w_ref.shape[0]
    ts = t_ref[...]
    deltas = []
    for b in range(blocks):
        rhs = c_ref[b] + tdot6(s_ref[b], ts) * inv_n
        for c in range(b):
            index, flip = pairs[(b, c)]
            dims = (((0,), (0,)), ((), ())) if flip else (((1,), (0,)), ((), ()))
            hi, lo = split(x_ref[index])
            rhs = rhs - (
                lax.dot_general(hi, deltas[c], dims, preferred_element_type=f32)
                + lax.dot_general(lo, deltas[c], dims, preferred_element_type=f32)
            )
        delta = dot6(w_ref[b], rhs)
        rounded = delta.astype(bf16)
        o_ref[b] = delta
        d_ref[b] = rounded
        deltas.append(rounded)
        s = s_ref[b]
        sh, sl = split(s)
        sm = (s - sh.astype(f32) - sl.astype(f32)).astype(bf16)
        ts = ts - (dot1(sh, rounded) + (dot1(sl, rounded) + dot1(sm, rounded)))


def solve(w, x, s, t, c, n, pairs):
    blocks, width, targets = c.shape
    parts = s.shape[1]
    tile = min(targets, 256)
    return pl.pallas_call(
        functools.partial(solve_kernel, 1.0 / n, pairs),
        grid=(targets // tile,),
        in_specs=[
            pl.BlockSpec(w.shape, lambda i: (0, 0, 0)),
            pl.BlockSpec(x.shape, lambda i: (0, 0, 0)),
            pl.BlockSpec(s.shape, lambda i: (0, 0, 0)),
            pl.BlockSpec((parts, tile), lambda i: (0, i)),
            pl.BlockSpec((blocks, width, tile), lambda i: (0, 0, i)),
        ],
        out_specs=[
            pl.BlockSpec((blocks, width, tile), lambda i: (0, 0, i)),
            pl.BlockSpec((blocks, width, tile), lambda i: (0, 0, i)),
        ],
        out_shape=[jax.ShapeDtypeStruct(c.shape, f32), jax.ShapeDtypeStruct(c.shape, bf16)],
        compiler_params=pltpu.CompilerParams(vmem_limit_bytes=VMEM),
        name="solve",
    )(w, x, s, t, c)


def fit_kernel(f_ref, d_ref, t_ref, o_ref):
    total = t_ref[...].astype(f32)
    for b in range(f_ref.shape[0]):
        total = total - dot1(f_ref[b], d_ref[b])
    o_ref[...] = total


def fit(feats, delta, targets):
    blocks, rows, width = feats.shape
    columns = targets.shape[1]
    tile = min(rows, 256)
    return pl.pallas_call(
        fit_kernel,
        grid=(rows // tile,),
        in_specs=[
            pl.BlockSpec((blocks, tile, width), lambda i: (0, i, 0)),
            pl.BlockSpec(delta.shape, lambda i: (0, 0, 0)),
            pl.BlockSpec((tile, columns), lambda i: (i, 0)),
        ],
        out_specs=pl.BlockSpec((tile, columns), lambda i: (i, 0)),
        out_shape=jax.ShapeDtypeStruct((rows, columns), f32),
        compiler_params=pltpu.CompilerParams(vmem_limit_bytes=VMEM),
        name="fit",
    )(feats, delta, targets)


def flip_pairs(bit):
    return [(i, i ^ (1 << bit)) for i in range(lax.axis_size("rows"))]


def reduce_scatter(x, order, scale):
    me = lax.axis_index("rows")
    for bit in order:
        mine = (me >> bit) & 1
        half = x.shape[0] // 2
        send = lax.dynamic_slice_in_dim(x, (1 - mine) * half, half)
        keep = lax.dynamic_slice_in_dim(x, mine * half, half)
        got = lax.ppermute((send * scale).astype(wire), "rows", flip_pairs(bit))
        x = keep + got.astype(f32) * (1.0 / scale)
    return x


def all_gather(x, order):
    me = lax.axis_index("rows")
    for bit in order[::-1]:
        mine = (me >> bit) & 1
        got = lax.ppermute(x, "rows", flip_pairs(bit))
        x = jnp.where(mine == 1, jnp.concatenate([got, x]), jnp.concatenate([x, got]))
    return x


def swap(x):
    cores = lax.axis_size("blk")
    return lax.ppermute(x, "blk", [(i, (i + 1) % cores) for i in range(cores)])


def tdot(a, b):
    return lax.dot_general(a, b, (((0,), (0,)), ((), ())), preferred_element_type=f32)


def body(inputs, proj, phase, targets):
    parts = lax.axis_size("rows")
    core = lax.axis_index("blk")
    n = inputs.shape[0]
    columns = targets.shape[1]
    owned, _, width = proj.shape
    scale = 1.0 / math.sqrt(n * parts)
    gscale = 2.0**15
    cscale = 2.0 ** math.floor(math.log2(65504.0 / (8.0 * math.sqrt(n * parts))))
    bits = list(range(parts.bit_length() - 1))
    order_a = bits
    order_b = [1, 2, 0] + bits[3:]
    order_c = [2, 0, 1] + bits[3:]

    proj2, phase2 = swap(proj), swap(phase)
    own = features(inputs, proj, phase, scale)
    own_sum = jnp.sum(own.astype(f32), axis=1)
    rank1 = lambda a, b: a[:, None] * (b * (1.0 / n))[None, :]
    diag = jnp.concatenate([tdot(own[i], own[i]) - rank1(own_sum[i], own_sum[i]) for i in range(owned)])
    diag = reduce_scatter(diag, order_a, gscale)

    other = features(inputs, proj2, phase2, scale)
    other_sum = jnp.sum(other.astype(f32), axis=1)
    tsum = jnp.sum(targets.astype(f32), axis=0)
    feats = jnp.concatenate([own, other])
    sums = jnp.concatenate([own_sum, other_sum])
    corr = jnp.concatenate([tdot(feats[i], targets) - rank1(sums[i], tsum) for i in range(2 * owned)])
    corr = reduce_scatter(corr, order_b, cscale)
    left = [own[1], other[core], other[1 - core]]
    left_sum = [own_sum[1], other_sum[core], other_sum[1 - core]]
    right = [own[0], own[0], own[1]]
    right_sum = [own_sum[0], own_sum[0], own_sum[1]]
    cross = jnp.concatenate([tdot(a, b) - rank1(p, q) for a, b, p, q in zip(left, right, left_sum, right_sum)])
    cross = reduce_scatter(cross, order_c, gscale)

    extra = jnp.concatenate([sums, tsum.reshape(-1, width)])
    high = extra.astype(wire)
    low = (extra - high.astype(f32)).astype(wire)
    extra = jnp.concatenate([high, low])
    extra = jnp.pad(extra, ((0, -extra.shape[0] % 16), (0, 0)))
    piece = diag.shape[0]
    got = all_gather(jnp.concatenate([(diag * gscale).astype(wire), extra]), order_a).reshape(parts, -1, width)
    gram = got[:, :piece].reshape(owned, width, width).astype(f32) * (1.0 / gscale)
    count = 2 * owned + columns // width
    extra = got[:, piece : piece + count].astype(f32) + got[:, piece + count : piece + 2 * count].astype(f32)
    sums = extra[:, : 2 * owned].transpose(1, 0, 2)
    tsums = extra[:, 2 * owned :].reshape(parts, columns)
    mine = factor(gram, sums[:owned], n)

    corr = all_gather((corr * cscale).astype(wire), order_b).reshape(2 * owned, width, columns).astype(f32) * (1.0 / cscale)
    cross = all_gather((cross * gscale).astype(wire), order_c)
    cross2 = swap(cross)
    theirs = swap(mine)
    first = core == 0
    both = lambda a, b: jnp.concatenate([jnp.where(first, a, b), jnp.where(first, b, a)])
    cross = both(cross, cross2).astype(f32).reshape(-1, width, width) * (1.0 / gscale)
    inverse = both(mine, theirs)
    sums = both(sums[:owned], sums[owned:])
    corr = both(corr[:owned], corr[owned:])
    pairs = {(1, 0): (0, False), (2, 0): (1, False), (3, 1): (2, False), (3, 2): (3, False), (2, 1): (4, True), (3, 0): (5, True)}
    coefs, delta = solve(inverse, cross, sums, tsums, corr, n, pairs)
    delta = jnp.where(first, delta, jnp.concatenate([delta[owned:], delta[:owned]]))
    residual = fit(feats, delta, targets)
    return (coefs, residual)


def solution(mesh):
    return jax.shard_map(
        body,
        mesh=mesh,
        in_specs=(P("rows", None), P("blk", None, None), P("blk", None), P("rows", "blk")),
        out_specs=(P(None, None, "blk"), P("rows", "blk")),
        check_vma=False,
    )
```

time: 870 us -> 286 us (0.33)
  other arithmetic: 337 us -> 34.9 us
  waiting for transfers between devices: 371 us -> 117 us
  Pallas kernels: 0 us -> 70.6 us
  matrix products: 80.8 us -> 11 us
  local copies, waits for them, and re-layouts: 52.2 us -> 6.48 us
  starting transfers between devices: 1.23 us -> 39.3 us
  between operations: 20.7 us -> 1.65 us
    psum x5 -> x0, waiting for transfers between devices: 358 us -> none  [the longest x4 330 us: body(): corr = lax.psum(partial_corr, 'rows')]
    another operation x44 -> x0, other arithmetic: 332 us -> none  [the longest x6 163 us: body(): delta = jax.scipy.linalg.cho_solve((factor, True), corr)]
    ppermute x0 -> x28, waiting for transfers between devices: none -> 117 us  [the longest x12 72.6 us: all_gather(): got = lax.ppermute(x, 'rows', flip_pairs(bit))]
    pallas_call x0 -> x5, Pallas kernels: none -> 70.6 us  [the longest x1 30.8 us: solve(): pl.pallas_call(functools.partial(solve_kernel, 1.0 / n, pairs), grid=(tar...]
    another operation x68 -> x0, matrix products: 45.3 us -> none  [the longest x56 34.4 us: body(): delta = jax.scipy.linalg.cho_solve((factor, True), corr)]
    another operation x61 -> x0, local copies, waits for them, and re-layouts: 42.7 us -> none  [the longest x53 42.4 us: body(): delta = jax.scipy.linalg.cho_solve((factor, True), corr)]
    ppermute x0 -> x28, starting transfers between devices: none -> 39.3 us  [the longest x12 19.7 us: reduce_scatter(): got = lax.ppermute((send * scale).astype(wire), 'rows', flip_pairs(bit))]
    dot_general x12 -> x9, matrix products: 35.5 us -> 11 us  [tdot(): lax.dot_general(a, b, (((0,), (0,)), ((), ())), preferred_element_type=f32)]
  transfers between devices with their start and end apart: 6 -> 28, of which waited for: 6 -> 15; matrix products, arithmetic and copies ran while one was open for 19% -> 15% of each run, Pallas kernels for 0% -> 12%
where the time goes in v1:
time: 286 us; the launch traced here: 281 us
  waiting for transfers between devices  117 us (41%)
  Pallas kernels  70.6 us (25%)
  starting transfers between devices  39.3 us (14%)
  other arithmetic  34.9 us (12%)
  matrix products  11 us (4%)
  local copies, waits for them, and re-layouts  6.48 us (2%)
    ppermute x12, waiting for transfers between devices, all_gather(): got = lax.ppermute(x, 'rows', flip_pairs(bit))  72.6 us
    ppermute x12, waiting for transfers between devices, reduce_scatter(): got = lax.ppermute((send * scale).astype(wire), 'rows', flip_pairs(bit))  44.2 us
    pallas_call x1, Pallas kernels, solve(): pl.pallas_call(functools.partial(solve_kernel, 1.0 / n, pairs), grid=(tar...  30.8 us
    pallas_call x1, Pallas kernels, factor(): pl.pallas_call(functools.partial(factor_kernel, 1.0 / n), out_shape=jax.S...  21.2 us
    ppermute x12, starting transfers between devices, reduce_scatter(): got = lax.ppermute((send * scale).astype(wire), 'rows', flip_pairs(bit))  19.7 us
    ppermute x12, starting transfers between devices, all_gather(): got = lax.ppermute(x, 'rows', flip_pairs(bit))  18.9 us
    pallas_call x2, Pallas kernels, features(): pl.pallas_call(functools.partial(features_kernel, scale), grid=(blocks, r...  12.9 us
    dot_general x9, matrix products, tdot(): lax.dot_general(a, b, (((0,), (0,)), ((), ())), preferred_element_type=f32)  11 us
  transfers between devices with their start and end apart: 28, of which 15 were waited for; matrix products, arithmetic and copies ran while one was open for 15% of the time, Pallas kernels for 12%

profile of v1, /device:TPU:0, one launch (start us, length us, event | category | flops | bytes accessed | tf_op | source)
XLA Modules:
  0.0 280.7 jit_solution(8964445046910104680)
XLA Ops:
  4.6 5.7 %features.2 = bf16[2,1024,512]{2,1,0:T(8,128)(2,1)S(1)} custom-call(bf16[1024,440]{1,0:T(8,128)(2,1)S(1)} %copy.8.x_ref, bf16[2,440,512]{2,1,0:T(8,128)(2,1)S(1)} %copy-done.4, bf16[2,1,512]{2,1,0:T(2,128)(2,1)S(1)} %copy.9.p_ref), custom_call_target="tpu_custom_call" | custom-call | tf_op jit(solution)/shard_map/features/pallas_call | solution.py:43
  14.3 2.9 %collective-permute-start = (f16[512,512]{1,0:T(8,128)(2,1)}, f16[512,512]{1,0:T(8,128)(2,1)}, u32[]{:S(2)}, u32[]{:S(2)}) collective-permute-start(f16[512,512]{1,0:T(8,128)(2,1)} %fusion.2), channel_id=1, source_target_pairs={{0,2},{2,0},{4,6},{6,4},{8,10},{10,8},{12,14},{14,12},{16,18},{18,... | collective-permute-start | bytes 1572872 | tf_op jit(solution)/shard_map/ppermute | solution.py:234
  20.5 3.1 %convolution_subtract_fusion.2 = f32[512,512]{1,0:T(8,128)} fusion(bf16[1024,512]{1,0:T(8,128)(2,1)} %t_ref.1, bf16[2,1024,512]{2,1,0:T(8,128)(2,1)S(1)} %features.2, f32[512]{0:T(512)S(1)} %broadcast_multiply_fusion, f32[512]{0:T(512)S(1)} %bitcast.70), kind=kOutput, calls=%fused_computation.28 | convolution fusion | flops 537395200 | bytes 3149824 | tf_op jit(solution)/shard_map/dot_general | solution.py:254
  23.5 6.2 %collective-permute-done = f16[512,512]{1,0:T(8,128)(2,1)} collective-permute-done((f16[512,512]{1,0:T(8,128)(2,1)}, f16[512,512]{1,0:T(8,128)(2,1)}, u32[]{:S(2)}, u32[]{:S(2)}) %collective-permute-start) | collective-permute-done | bytes 524320 | tf_op jit(solution)/shard_map/ppermute | solution.py:234
  36.4 4.5 %collective-permute-done.1 = f16[256,512]{1,0:T(8,128)(2,1)S(1)} collective-permute-done((f16[256,512]{1,0:T(8,128)(2,1)}, f16[256,512]{1,0:T(8,128)(2,1)S(1)}, u32[]{:S(2)}, u32[]{:S(2)}) %collective-permute-start.1) | collective-permute-done | bytes 262176 | tf_op jit(solution)/shard_map/ppermute | solution.py:234
  43.7 7.2 %features.3 = bf16[2,1024,512]{2,1,0:T(8,128)(2,1)S(1)} custom-call(bf16[1024,440]{1,0:T(8,128)(2,1)S(1)} %copy.8.x_ref, bf16[2,440,512]{2,1,0:T(8,128)(2,1)} %collective-permute-done.4.w_ref, bf16[2,1,512]{2,1,0:T(2,128)(2,1)S(1)} %copy.11.p_ref), custom_call_target="tpu_custom_call" | custom-call | tf_op jit(solution)/shard_map/features/pallas_call | solution.py:43
  57.3 2.6 collective-permute-start.3
  59.9 14.2 %collective-permute-done.3 = f16[64,512]{1,0:T(8,128)(2,1)S(1)} collective-permute-done((f16[64,512]{1,0:T(8,128)(2,1)S(1)}, f16[64,512]{1,0:T(8,128)(2,1)S(1)}, u32[]{:S(2)}, u32[]{:S(2)}) %collective-permute-start.3) | collective-permute-done | bytes 65568 | tf_op jit(solution)/shard_map/ppermute | solution.py:234
  74.2 3.4 %collective-permute-start.6 = (f16[80,512]{1,0:T(8,128)(2,1)S(1)}, f16[80,512]{1,0:T(8,128)(2,1)S(1)}, u32[]{:S(2)}, u32[]{:S(2)}) collective-permute-start(f16[80,512]{1,0:T(8,128)(2,1)S(1)} %pad_maximum_fusion.6), channel_id=1, source_target_pairs={{0,16},{2,18},{4,20},{6,22},{8,24},{10,26},{12,28},{14,30},{16,0},... | collective-permute-start | bytes 245768 | tf_op jit(solution)/shard_map/ppermute | solution.py:243
  80.3 4.4 %collective-permute-start.7 = (f16[160,512]{1,0:T(8,128)(2,1)S(1)}, f16[160,512]{1,0:T(8,128)(2,1)}, u32[]{:S(2)}, u32[]{:S(2)}) collective-permute-start(f16[160,512]{1,0:T(8,128)(2,1)S(1)} %maximum_select_fusion.12), channel_id=1, source_target_pairs={{0,8},{2,10},{4,12},{6,14},{8,0},{10,2},{12,4},{14,6},{16,24},{18,... | collective-permute-start | bytes 491528 | tf_op jit(solution)/shard_map/ppermute | solution.py:243
  90.6 22.6 %collective-permute-done.8 = f16[320,512]{1,0:T(8,128)(2,1)} collective-permute-done((f16[320,512]{1,0:T(8,128)(2,1)S(1)}, f16[320,512]{1,0:T(8,128)(2,1)}, u32[]{:S(2)}, u32[]{:S(2)}) %collective-permute-start.8) | collective-permute-done | bytes 327712 | tf_op jit(solution)/shard_map/ppermute | solution.py:243
  121.2 12.5 %collective-permute-done.12 = f16[384,512]{1,0:T(8,128)(2,1)S(1)} collective-permute-done((f16[384,512]{1,0:T(8,128)(2,1)S(1)}, f16[384,512]{1,0:T(8,128)(2,1)S(1)}, u32[]{:S(2)}, u32[]{:S(2)}) %collective-permute-start.12) | collective-permute-done | bytes 393248 | tf_op jit(solution)/shard_map/ppermute | solution.py:234
  143.1 5.1 %collective-permute-done.14 = f16[96,512]{1,0:T(8,128)(2,1)S(1)} collective-permute-done((f16[96,512]{1,0:T(8,128)(2,1)S(1)}, f16[96,512]{1,0:T(8,128)(2,1)S(1)}, u32[]{:S(2)}, u32[]{:S(2)}) %collective-permute-start.14) | collective-permute-done | bytes 98336 | tf_op jit(solution)/shard_map/ppermute | solution.py:234
  148.5 3.0 %collective-permute-start.23 = (f16[128,512]{1,0:T(8,128)(2,1)S(1)}, f16[128,512]{1,0:T(8,128)(2,1)S(1)}, u32[]{:S(2)}, u32[]{:S(2)}) collective-permute-start(f16[128,512]{1,0:T(8,128)(2,1)S(1)} %multiply_convert_fusion.8), channel_id=1, source_target_pairs={{0,16},{2,18},{4,20},{6,22},{8,24},{10,26},{12,28},{14,30},{16,0},... | collective-permute-start | bytes 393224 | tf_op jit(solution)/shard_map/ppermute | solution.py:234
  151.5 21.2 %factor.1 = f32[2,512,512]{2,1,0:T(8,128)S(1)} custom-call(f32[2,512,512]{2,1,0:T(8,128)} %bitcast.49, f32[2,16,512]{2,1,0:T(8,128)S(1)} %get-tuple-element.18.s_ref), custom_call_target="tpu_custom_call" | custom-call | tf_op jit(solution)/shard_map/factor/pallas_call | solution.py:139
  174.5 5.7 %collective-permute-done.16 = f16[192,512]{1,0:T(8,128)(2,1)S(1)} collective-permute-done((f16[192,512]{1,0:T(8,128)(2,1)S(1)}, f16[192,512]{1,0:T(8,128)(2,1)S(1)}, u32[]{:S(2)}, u32[]{:S(2)}) %collective-permute-start.16) | collective-permute-done | bytes 196640 | tf_op jit(solution)/shard_map/ppermute | solution.py:243
  184.6 12.2 %collective-permute-done.25 = f16[256,512]{1,0:T(8,128)(2,1)S(1)} collective-permute-done((f16[256,512]{1,0:T(8,128)(2,1)S(1)}, f16[256,512]{1,0:T(8,128)(2,1)S(1)}, u32[]{:S(2)}, u32[]{:S(2)}) %collective-permute-start.25) | collective-permute-done | bytes 262176 | tf_op jit(solution)/shard_map/ppermute | solution.py:243
  202.0 10.0 %collective-permute-done.26 = f16[512,512]{1,0:T(8,128)(2,1)S(1)} collective-permute-done((f16[512,512]{1,0:T(8,128)(2,1)S(1)}, f16[512,512]{1,0:T(8,128)(2,1)S(1)}, u32[]{:S(2)}, u32[]{:S(2)}) %collective-permute-start.26) | collective-permute-done | bytes 524320 | tf_op jit(solution)/shard_map/ppermute | solution.py:243
  213.9 12.7 %collective-permute-done.18 = f16[768,512]{1,0:T(8,128)(2,1)S(1)} collective-permute-done((f16[768,512]{1,0:T(8,128)(2,1)S(1)}, f16[768,512]{1,0:T(8,128)(2,1)S(1)}, u32[]{:S(2)}, u32[]{:S(2)}) %collective-permute-start.18) | collective-permute-done | bytes 786464 | tf_op jit(solution)/shard_map/ppermute | solution.py:243
  227.9 5.4 %collective-permute-done.27 = f16[1024,512]{1,0:T(8,128)(2,1)S(1)} collective-permute-done((f16[1024,512]{1,0:T(8,128)(2,1)S(1)}, f16[1024,512]{1,0:T(8,128)(2,1)S(1)}, u32[]{:S(2)}, u32[]{:S(2)}) %collective-permute-start.27) | collective-permute-done | bytes 1048608 | tf_op jit(solution)/shard_map/ppermute | solution.py:243
  234.7 4.3 %pad_maximum_fusion = (f32[4,512,512]{2,1,0:T(8,128)}, f32[4,512,512]{2,1,0:T(8,128)}) fusion(f32[2,512,512]{2,1,0:T(8,128)S(1)} %get-tuple-element.9, f32[2,512,512]{2,1,0:T(8,128)S(1)} %get-tuple-element.8, f32[2,512,512]{2,1,0:T(8,128)S(1)} %bitcast.51, f32[2,512,512]{2,1,0:T(8,128)S(1)} %bitcast.50), kind=kLoop, calls=%fused_computation.1 | loop fusion | flops 2097152 | bytes 16777216 | tf_op jit(solution)/shard_map/concatenate | solution.py:311
  239.7 3.7 %convert_multiply_fusion = f32[3072,512]{1,0:T(8,128)} fusion(f16[1536,512]{1,0:T(8,128)(2,1)S(1)} %get-tuple-element.11, f16[1536,512]{1,0:T(8,128)(2,1)S(1)} %get-tuple-element.10), kind=kLoop, calls=%fused_computation | loop fusion | flops 4718592 | bytes 9437184 | tf_op jit(solution)/shard_map/mul | solution.py:312
  243.3 30.8 %solve.1 = (f32[4,512,512]{2,1,0:T(8,128)}, bf16[4,512,512]{2,1,0:T(8,128)(2,1)S(1)}) custom-call(f32[4,512,512]{2,1,0:T(8,128)} %get-tuple-element.29.w_ref, f32[6,512,512]{2,1,0:T(8,128)} %bitcast.48, f32[4,16,512]{2,1,0:T(8,128)S(1)} %pad_maximum_fusion.5.s_ref, f32[16,512]{1,0:T(8,128)S(1)} %slice_bitcast_fusion.15.t_ref, ...), custom_call_target="tpu_custom_call" | custom-call | tf_op jit(solution)/shard_map/solve/pallas_call | solution.py:177
  274.6 5.7 %fit.1 = f32[1024,512]{1,0:T(8,128)} custom-call(bf16[4,1024,512]{2,1,0:T(8,128)(2,1)} %pad_maximum_fusion.3.f_ref, bf16[4,512,512]{2,1,0:T(8,128)(2,1)S(1)} %maximum_select_fusion.1.d_ref, bf16[1024,512]{1,0:T(8,128)(2,1)S(1)} %copy-done.3), custom_call_target="tpu_custom_call" | custom-call | tf_op jit(solution)/shard_map/fit/pallas_call | solution.py:208
  (145 shorter events, 70.1 us)
Async XLA Ops:
  0.6 35.8 %collective-permute-start.5 = (bf16[2,512]{1,0:T(2,128)(2,1)}, bf16[2,512]{1,0:T(2,128)(2,1)S(1)}, u32[]{:S(2)}, u32[]{:S(2)}) collective-permute-start(bf16[2,512]{1,0:T(2,128)(2,1)} %param.6), channel_id=1, source_target_pairs={{0,1},{1,0},{2,3},{3,2},{4,5},{5,4},{6,7},{7,6},{8,9},{9,8},{10,11... | collective-permute-start | bytes 6152 | tf_op jit(solution)/shard_map/ppermute | solution.py:250
  1.1 42.5 %collective-permute-start.4 = (bf16[2,440,512]{2,1,0:T(8,128)(2,1)}, bf16[2,440,512]{2,1,0:T(8,128)(2,1)}, u32[]{:S(2)}, u32[]{:S(2)}) collective-permute-start(bf16[2,440,512]{2,1,0:T(8,128)(2,1)} %w_ref.1), channel_id=1, source_target_pairs={{0,1},{1,0},{2,3},{3,2},{4,5},{5,4},{6,7},{7,6},{8,9},{9,8},{10,11... | collective-permute-start | bytes 2703368 | tf_op jit(solution)/shard_map/ppermute | solution.py:250
  14.3 15.4 %collective-permute-start = (f16[512,512]{1,0:T(8,128)(2,1)}, f16[512,512]{1,0:T(8,128)(2,1)}, u32[]{:S(2)}, u32[]{:S(2)}) collective-permute-start(f16[512,512]{1,0:T(8,128)(2,1)} %fusion.2), channel_id=1, source_target_pairs={{0,2},{2,0},{4,6},{6,4},{8,10},{10,8},{12,14},{14,12},{16,18},{18,... | collective-permute-start | bytes 1572872 | tf_op jit(solution)/shard_map/ppermute | solution.py:234
  32.9 8.0 %collective-permute-start.1 = (f16[256,512]{1,0:T(8,128)(2,1)}, f16[256,512]{1,0:T(8,128)(2,1)S(1)}, u32[]{:S(2)}, u32[]{:S(2)}) collective-permute-start(f16[256,512]{1,0:T(8,128)(2,1)} %multiply_convert_fusion.5), channel_id=1, source_target_pairs={{0,4},{2,6},{4,0},{6,2},{8,12},{10,14},{12,8},{14,10},{16,20},{18,... | collective-permute-start | bytes 786440 | tf_op jit(solution)/shard_map/ppermute | solution.py:234
  42.1 15.1 %collective-permute-start.2 = (f16[128,512]{1,0:T(8,128)(2,1)S(1)}, f16[128,512]{1,0:T(8,128)(2,1)S(1)}, u32[]{:S(2)}, u32[]{:S(2)}) collective-permute-start(f16[128,512]{1,0:T(8,128)(2,1)S(1)} %multiply_convert_fusion.9), channel_id=1, source_target_pairs={{0,8},{2,10},{4,12},{6,14},{8,0},{10,2},{12,4},{14,6},{16,24},{18,... | collective-permute-start | bytes 393224 | tf_op jit(solution)/shard_map/ppermute | solution.py:234
  56.7 59.4 %collective-permute-start.11 = (f16[768,512]{1,0:T(8,128)(2,1)}, f16[768,512]{1,0:T(8,128)(2,1)}, u32[]{:S(2)}, u32[]{:S(2)}) collective-permute-start(f16[768,512]{1,0:T(8,128)(2,1)} %multiply_convert_fusion.1), channel_id=1, source_target_pairs={{0,8},{2,10},{4,12},{6,14},{8,0},{10,2},{12,4},{14,6},{16,24},{18,... | collective-permute-start | bytes 2359304 | tf_op jit(solution)/shard_map/ppermute | solution.py:234
  57.3 16.8 %collective-permute-start.3 = (f16[64,512]{1,0:T(8,128)(2,1)S(1)}, f16[64,512]{1,0:T(8,128)(2,1)S(1)}, u32[]{:S(2)}, u32[]{:S(2)}) collective-permute-start(f16[64,512]{1,0:T(8,128)(2,1)S(1)} %multiply_convert_fusion.13), channel_id=1, source_target_pairs={{0,16},{2,18},{4,20},{6,22},{8,24},{10,26},{12,28},{14,30},{16,0},... | collective-permute-start | bytes 196616 | tf_op jit(solution)/shard_map/ppermute | solution.py:234
  80.3 7.8 %collective-permute-start.7 = (f16[160,512]{1,0:T(8,128)(2,1)S(1)}, f16[160,512]{1,0:T(8,128)(2,1)}, u32[]{:S(2)}, u32[]{:S(2)}) collective-permute-start(f16[160,512]{1,0:T(8,128)(2,1)S(1)} %maximum_select_fusion.12), channel_id=1, source_target_pairs={{0,8},{2,10},{4,12},{6,14},{8,0},{10,2},{12,4},{14,6},{16,24},{18,... | collective-permute-start | bytes 491528 | tf_op jit(solution)/shard_map/ppermute | solution.py:243
  85.9 33.2 %collective-permute-start.20 = (f16[1024,512]{1,0:T(8,128)(2,1)}, f16[1024,512]{1,0:T(8,128)(2,1)}, u32[]{:S(2)}, u32[]{:S(2)}) collective-permute-start(f16[1024,512]{1,0:T(8,128)(2,1)} %multiply_convert_fusion), channel_id=1, source_target_pairs={{0,4},{2,6},{4,0},{6,2},{8,12},{10,14},{12,8},{14,10},{16,20},{18,... | collective-permute-start | bytes 3145736 | tf_op jit(solution)/shard_map/ppermute | solution.py:234
  89.3 23.9 %collective-permute-start.8 = (f16[320,512]{1,0:T(8,128)(2,1)S(1)}, f16[320,512]{1,0:T(8,128)(2,1)}, u32[]{:S(2)}, u32[]{:S(2)}) collective-permute-start(f16[320,512]{1,0:T(8,128)(2,1)S(1)} %maximum_select_fusion.9), channel_id=1, source_target_pairs={{0,4},{2,6},{4,0},{6,2},{8,12},{10,14},{12,8},{14,10},{16,20},{18,... | collective-permute-start | bytes 983048 | tf_op jit(solution)/shard_map/ppermute | solution.py:243
  114.6 21.0 %collective-permute-start.9 = (f16[640,512]{1,0:T(8,128)(2,1)S(1)}, f16[640,512]{1,0:T(8,128)(2,1)S(1)}, u32[]{:S(2)}, u32[]{:S(2)}) collective-permute-start(f16[640,512]{1,0:T(8,128)(2,1)S(1)} %maximum_select_fusion.6), channel_id=1, source_target_pairs={{0,2},{2,0},{4,6},{6,4},{8,10},{10,8},{12,14},{14,12},{16,18},{18,... | collective-permute-start | bytes 1966088 | tf_op jit(solution)/shard_map/ppermute | solution.py:243
  118.1 15.6 %collective-permute-start.12 = (f16[384,512]{1,0:T(8,128)(2,1)S(1)}, f16[384,512]{1,0:T(8,128)(2,1)S(1)}, u32[]{:S(2)}, u32[]{:S(2)}) collective-permute-start(f16[384,512]{1,0:T(8,128)(2,1)S(1)} %multiply_convert_fusion.3), channel_id=1, source_target_pairs={{0,2},{2,0},{4,6},{6,4},{8,10},{10,8},{12,14},{14,12},{16,18},{18,... | collective-permute-start | bytes 1179656 | tf_op jit(solution)/shard_map/ppermute | solution.py:234
  120.9 20.8 %collective-permute-start.21 = (f16[512,512]{1,0:T(8,128)(2,1)S(1)}, f16[512,512]{1,0:T(8,128)(2,1)S(1)}, u32[]{:S(2)}, u32[]{:S(2)}) collective-permute-start(f16[512,512]{1,0:T(8,128)(2,1)S(1)} %multiply_convert_fusion.2), channel_id=1, source_target_pairs={{0,8},{2,10},{4,12},{6,14},{8,0},{10,2},{12,4},{14,6},{16,24},{18,... | collective-permute-start | bytes 1572872 | tf_op jit(solution)/shard_map/ppermute | solution.py:234
  139.7 8.5 %collective-permute-start.14 = (f16[96,512]{1,0:T(8,128)(2,1)S(1)}, f16[96,512]{1,0:T(8,128)(2,1)S(1)}, u32[]{:S(2)}, u32[]{:S(2)}) collective-permute-start(f16[96,512]{1,0:T(8,128)(2,1)S(1)} %multiply_convert_fusion.11), channel_id=1, source_target_pairs={{0,16},{2,18},{4,20},{6,22},{8,24},{10,26},{12,28},{14,30},{16,0},... | collective-permute-start | bytes 294920 | tf_op jit(solution)/shard_map/ppermute | solution.py:234
  148.2 24.5 %collective-permute-start.15 = (f16[96,512]{1,0:T(8,128)(2,1)S(1)}, f16[96,512]{1,0:T(8,128)(2,1)S(1)}, u32[]{:S(2)}, u32[]{:S(2)}) collective-permute-start(f16[96,512]{1,0:T(8,128)(2,1)S(1)} %multiply_convert_fusion.10), channel_id=1, source_target_pairs={{0,16},{2,18},{4,20},{6,22},{8,24},{10,26},{12,28},{14,30},{16,0},... | collective-permute-start | bytes 294920 | tf_op jit(solution)/shard_map/ppermute | solution.py:243
  148.5 25.9 %collective-permute-start.23 = (f16[128,512]{1,0:T(8,128)(2,1)S(1)}, f16[128,512]{1,0:T(8,128)(2,1)S(1)}, u32[]{:S(2)}, u32[]{:S(2)}) collective-permute-start(f16[128,512]{1,0:T(8,128)(2,1)S(1)} %multiply_convert_fusion.8), channel_id=1, source_target_pairs={{0,16},{2,18},{4,20},{6,22},{8,24},{10,26},{12,28},{14,30},{16,0},... | collective-permute-start | bytes 393224 | tf_op jit(solution)/shard_map/ppermute | solution.py:234
  172.7 54.7 %collective-permute-start.10 = (f32[2,512,512]{2,1,0:T(8,128)S(1)}, f32[2,512,512]{2,1,0:T(8,128)S(1)}, u32[]{:S(2)}, u32[]{:S(2)}) collective-permute-start(f32[2,512,512]{2,1,0:T(8,128)S(1)} %factor.1), channel_id=1, source_target_pairs={{0,1},{1,0},{2,3},{3,2},{4,5},{5,4},{6,7},{7,6},{8,9},{9,8},{10,11... | collective-permute-start | bytes 6291464 | tf_op jit(solution)/shard_map/ppermute | solution.py:250
  174.4 8.5 %collective-permute-start.24 = (f16[128,512]{1,0:T(8,128)(2,1)S(1)}, f16[128,512]{1,0:T(8,128)(2,1)S(1)}, u32[]{:S(2)}, u32[]{:S(2)}) collective-permute-start(f16[128,512]{1,0:T(8,128)(2,1)S(1)} %multiply_convert_fusion.7), channel_id=1, source_target_pairs={{0,16},{2,18},{4,20},{6,22},{8,24},{10,26},{12,28},{14,30},{16,0},... | collective-permute-start | bytes 393224 | tf_op jit(solution)/shard_map/ppermute | solution.py:243
  180.4 16.7 %collective-permute-start.17 = (f16[384,512]{1,0:T(8,128)(2,1)S(1)}, f16[384,512]{1,0:T(8,128)(2,1)S(1)}, u32[]{:S(2)}, u32[]{:S(2)}) collective-permute-start(f16[384,512]{1,0:T(8,128)(2,1)S(1)} %maximum_select_fusion.8), channel_id=1, source_target_pairs={{0,2},{2,0},{4,6},{6,4},{8,10},{10,8},{12,14},{14,12},{16,18},{18,... | collective-permute-start | bytes 1179656 | tf_op jit(solution)/shard_map/ppermute | solution.py:243
  183.0 13.8 %collective-permute-start.25 = (f16[256,512]{1,0:T(8,128)(2,1)S(1)}, f16[256,512]{1,0:T(8,128)(2,1)S(1)}, u32[]{:S(2)}, u32[]{:S(2)}) collective-permute-start(f16[256,512]{1,0:T(8,128)(2,1)S(1)} %maximum_select_fusion.10), channel_id=1, source_target_pairs={{0,2},{2,0},{4,6},{6,4},{8,10},{10,8},{12,14},{14,12},{16,18},{18,... | collective-permute-start | bytes 786440 | tf_op jit(solution)/shard_map/ppermute | solution.py:243
  197.0 14.9 %collective-permute-start.26 = (f16[512,512]{1,0:T(8,128)(2,1)S(1)}, f16[512,512]{1,0:T(8,128)(2,1)S(1)}, u32[]{:S(2)}, u32[]{:S(2)}) collective-permute-start(f16[512,512]{1,0:T(8,128)(2,1)S(1)} %maximum_select_fusion.7), channel_id=1, source_target_pairs={{0,8},{2,10},{4,12},{6,14},{8,0},{10,2},{12,4},{14,6},{16,24},{18,... | collective-permute-start | bytes 1572872 | tf_op jit(solution)/shard_map/ppermute | solution.py:243
  197.5 29.1 %collective-permute-start.18 = (f16[768,512]{1,0:T(8,128)(2,1)S(1)}, f16[768,512]{1,0:T(8,128)(2,1)S(1)}, u32[]{:S(2)}, u32[]{:S(2)}) collective-permute-start(f16[768,512]{1,0:T(8,128)(2,1)S(1)} %maximum_select_fusion.5), channel_id=1, source_target_pairs={{0,8},{2,10},{4,12},{6,14},{8,0},{10,2},{12,4},{14,6},{16,24},{18,... | collective-permute-start | bytes 2359304 | tf_op jit(solution)/shard_map/ppermute | solution.py:243
  212.4 20.8 %collective-permute-start.27 = (f16[1024,512]{1,0:T(8,128)(2,1)S(1)}, f16[1024,512]{1,0:T(8,128)(2,1)S(1)}, u32[]{:S(2)}, u32[]{:S(2)}) collective-permute-start(f16[1024,512]{1,0:T(8,128)(2,1)S(1)} %maximum_select_fusion.4), channel_id=1, source_target_pairs={{0,4},{2,6},{4,0},{6,2},{8,12},{10,14},{12,8},{14,10},{16,20},{18,... | collective-permute-start | bytes 3145736 | tf_op jit(solution)/shard_map/ppermute | solution.py:243
  227.3 11.7 %collective-permute-start.19 = (f16[1536,512]{1,0:T(8,128)(2,1)S(1)}, f16[1536,512]{1,0:T(8,128)(2,1)S(1)}, u32[]{:S(2)}, u32[]{:S(2)}) collective-permute-start(f16[1536,512]{1,0:T(8,128)(2,1)S(1)} %maximum_select_fusion.2), channel_id=1, source_target_pairs={{0,1},{1,0},{2,3},{3,2},{4,5},{5,4},{6,7},{7,6},{8,9},{9,8},{10,11... | collective-permute-start | bytes 4718600 | tf_op jit(solution)/shard_map/ppermute | solution.py:250
  (21 other events, 172.9 us)
